TPU v7x, 32 devices: a whole 2x2x4 slice. The times are simulated.
32 devices in a mesh: slab: 32 (over z, y, x, core).
Axes of the slice: x: 2, y: 2, z: 4, core: 2. Of those that a mesh axis runs over, the one named last changes fastest.
Arguments:
- velocity: float32 [3, 256, 32, 128], P(None, 'slab'), may hold values from -6 to 6
- node_coords: float32 [4096, 3, 128], P('slab'), may hold values from 0 to 1
- node_force: float32 [4096, 3, 128], P('slab'), may hold values from -12 to 12
- block_slab: int32 [4096, 1], P('slab'), may hold values from 0 to 31; in each aligned block of 128 rows (0 to 127, 128 to 255, ...) at most 8 rows name the same one
- block_offset: int32 [4096, 2], P('slab'), may hold values from 1 to 25
Outputs:
- new_velocity: float32 [3, 256, 32, 128], P(None, 'slab')
- node_velocity: float32 [4096, 3, 128], P('slab')
Inputs may be any that keep to these rules, and one draw needn't show every extreme that they name: `block_slab`: among the 128 blocks of one device at most 8 name the same slab, and in every draw some device has exactly 8 blocks in one slab.
All inputs are finite; a program needn't handle non-finite values.
Results may differ from a plain program's by a relative error of at most 0.0003.
Values sent between devices are 32-bit elements; how exact they have to be, the bound alone decides.
A program may use at most 128 MiB of HBM per device.

v0:
```python
import math

import jax
import jax.numpy as jnp
from jax import lax
from jax.sharding import PartitionSpec as P

CX = 8
SUBSTEPS = 3


time_step = 0.1
viscosity = 0.2


def padded_2(cells, sides, width):
    for axis, dim in sides:
        count = lax.axis_size(axis)
        head = lax.slice_in_dim(cells, 0, width, axis=dim)
        tail = lax.slice_in_dim(cells, cells.shape[dim] - width, cells.shape[dim], axis=dim)
        cells = jnp.concatenate(
            [
                lax.ppermute(tail, axis, [(i, (i + 1) % count) for i in range(count)]),
                cells,
                lax.ppermute(head, axis, [((i + 1) % count, i) for i in range(count)]),
            ],
            axis=dim,
        )
    return cells


def kernel(distance):
    return jnp.where(jnp.abs(distance) < 2.0, 0.25 * (1.0 + jnp.cos(0.5 * math.pi * distance)), 0.0)


def node_weights(coords):
    planes = jnp.arange(CX, dtype=jnp.float32)
    taps = jnp.arange(8, dtype=jnp.float32)
    weight_x = kernel(planes[None, None, :] - 1.0 - (CX - 4) * coords[:, 0, :, None])
    weight_y = kernel(taps[None, None, :] - 1.0 - 5.0 * coords[:, 1, :, None])
    weight_z = kernel(taps[None, None, :] - 1.0 - 5.0 * coords[:, 2, :, None])
    count = coords.shape[0]
    nodes = coords.shape[2]
    joint = (weight_x[:, :, :, None] * weight_y[:, :, None, :]).reshape(count, nodes, CX * 8)
    return (joint, weight_z)


def make_patches(coords, force):
    count = coords.shape[0]
    nodes = coords.shape[2]
    joint, weight_z = node_weights(coords)
    force_z = (jnp.transpose(force, (0, 2, 1))[:, :, :, None] * weight_z[:, :, None, :]).reshape(
        count, nodes, 24
    )
    summed = jnp.einsum("knm,knq->kmq", joint, force_z, precision=lax.Precision.HIGHEST)
    summed = jnp.transpose(summed.reshape(count, CX, 8, 3, 8), (0, 3, 1, 2, 4))
    return summed.reshape(count, 3 * CX * 64)


def interpolate(flat, coords):
    count = coords.shape[0]
    joint, weight_z = node_weights(coords)
    values = flat.reshape(count, 3, CX * 8, 8)
    partial_sum = jnp.einsum("knm,kcmj->kncj", joint, values, precision=lax.Precision.HIGHEST)
    result = jnp.sum(partial_sum * weight_z[:, :, None, :], axis=3)
    return jnp.transpose(result, (0, 2, 1))


def grouped(function, arrays):
    count = arrays[0].shape[0]
    group = min(count, 128)
    shaped = tuple((a.reshape((count // group, group) + a.shape[1:]) for a in arrays))
    result = lax.map(lambda pieces: function(*pieces), shaped)
    return result.reshape((count,) + result.shape[2:])


def window_tables(offsets, rows_total, cols_total):
    taps = jnp.arange(8, dtype=jnp.int32)
    row_start = offsets[:, 0:1] - 1 + taps[None, :]
    col_start = offsets[:, 1:2] - 1 + taps[None, :]
    row_hot = (
        row_start[:, :, None] == jnp.arange(rows_total, dtype=jnp.int32)[None, None, :]
    ).astype(jnp.float32)
    col_hot = (
        col_start[:, :, None] == jnp.arange(cols_total, dtype=jnp.int32)[None, None, :]
    ).astype(jnp.float32)
    return (row_hot, col_hot)


def place(flat, offsets, template):
    count = flat.shape[0]
    rows_total = template.shape[2]
    cols_total = template.shape[3]
    group = min(count, 32)
    shaped_flat = flat.reshape(count // group, group, 3, CX, 8, 8)
    shaped_offsets = offsets.reshape(count // group, group, 2)

    def add_group(total, pieces):
        patch_group, offset_group = pieces
        row_hot, col_hot = window_tables(offset_group, rows_total, cols_total)
        partial_value = jnp.einsum(
            "kcaij,kjz->kicaz", patch_group, col_hot, precision=lax.Precision.HIGHEST
        )
        placed = jnp.einsum(
            "kiy,kicaz->cayz", row_hot, partial_value, precision=lax.Precision.HIGHEST
        )
        return (total + placed, None)

    start = jnp.zeros(template.shape, jnp.float32)
    total, unused = lax.scan(add_group, start, (shaped_flat, shaped_offsets))
    return total


def around_blocks(field, offsets):
    count = offsets.shape[0]
    rows_total = field.shape[2]
    cols_total = field.shape[3]
    group = min(count, 32)
    shaped_offsets = offsets.reshape(count // group, group, 2)

    def read_group(offset_group):
        row_hot, col_hot = window_tables(offset_group, rows_total, cols_total)
        partial_value = jnp.einsum(
            "cayz,kjz->kcayj", field, col_hot, precision=lax.Precision.HIGHEST
        )
        picked = jnp.einsum(
            "kiy,kcayj->kcaij", row_hot, partial_value, precision=lax.Precision.HIGHEST
        )
        return picked.reshape(group, 3 * CX * 64)

    result = lax.map(read_group, shaped_offsets)
    return result.reshape(count, 3 * CX * 64)


def fluid_step(padded, forcing):
    center = padded[:, 1:-1]
    ahead = padded[:, 2:]
    behind = padded[:, :-2]
    y_plus = jnp.roll(center, -1, 2)
    y_minus = jnp.roll(center, 1, 2)
    z_plus = jnp.roll(center, -1, 3)
    z_minus = jnp.roll(center, 1, 3)
    laplace = ahead + behind + y_plus + y_minus + z_plus + z_minus - 6.0 * center
    advect = (
        center[0:1] * (ahead - behind) * 0.5
        + center[1:2] * (y_plus - y_minus) * 0.5
        + center[2:3] * (z_plus - z_minus) * 0.5
    )
    return center + time_step * (viscosity * laplace - advect + forcing)


def advance(velocity, force_grid):
    field = velocity
    for substep in range(SUBSTEPS):
        padded = padded_2(field, (("slab", 1),), 1)
        field = fluid_step(padded, force_grid)
    return field


def body(velocity, node_coords, node_force, block_slab, block_offset):
    devices = lax.axis_size("slab")
    count = node_coords.shape[0]
    capacity = 2 * count // devices
    slot_total = devices * capacity
    target_slab = block_slab[:, 0]
    one_hot = (target_slab[:, None] == jnp.arange(devices, dtype=jnp.int32)[None, :]).astype(
        jnp.int32
    )
    earlier = jnp.cumsum(one_hot, axis=0) - one_hot
    position_rank = jnp.sum(earlier * one_hot, axis=1)
    slot_index = target_slab * capacity + position_rank
    send_offsets = jnp.ones((slot_total, 2), jnp.int32).at[slot_index].set(block_offset)
    patches = grouped(make_patches, (node_coords, node_force))
    send_patches = (
        jnp.zeros((slot_total, patches.shape[1]), jnp.float32).at[slot_index].set(patches)
    )
    got_patches, got_offsets = (
        lax.all_to_all(send_patches, "slab", split_axis=0, concat_axis=0, tiled=True),
        lax.all_to_all(send_offsets, "slab", split_axis=0, concat_axis=0, tiled=True),
    )
    force_grid = place(got_patches, got_offsets, velocity)
    field = advance(velocity, force_grid)
    local_values = around_blocks(field, got_offsets)
    returned = lax.all_to_all(local_values, "slab", split_axis=0, concat_axis=0, tiled=True)
    node_velocity = grouped(interpolate, (returned[slot_index], node_coords))
    return (field, node_velocity)


def solution(mesh):
    return jax.shard_map(
        body,
        mesh=mesh,
        in_specs=(
            P(None, "slab", None, None),
            P("slab", None, None),
            P("slab", None, None),
            P("slab", None),
            P("slab", None),
        ),
        out_specs=(P(None, "slab", None, None), P("slab", None, None)),
        check_vma=False,
    )
```

profile of v0, /device:TPU:0, one launch (start us, length us, event | category | flops | bytes accessed | tf_op | source)
XLA Modules:
  0.0 276.8 jit_solution(11377972461282639657)
XLA Ops:
  5.6 7.3 %all-to-all-start = ((s32[32,8,2]{1,2,0:T(2,128)}), s32[32,8,2]{1,2,0:T(2,128)S(1)}, u32[]{:S(2)}, u32[]{:S(2)}) async-start(s32[32,8,2]{1,2,0:T(2,128)} %copy.36), calls=%async_computation | async-start | bytes 65536 | tf_op jit(solution)/shard_map/all_to_all | solution.py:179
  14.9 5.3 %fusion.61 = (f32[128,128,8]{1,2,0:T(8,128)S(1)}, f32[128,128,8]{1,2,0:T(8,128)S(1)}, f32[128,128,8]{1,2,0:T(8,128)S(1)}) fusion(f32[128,128]{1,0:T(8,128)S(1)} %get-tuple-element.266, f32[8]{0:T(128)S(1)} %iota_add_fusion.4, f32[128,128]{1,0:T(8,128)S(1)} %get-tuple-element.268, f32[128,128]{1,0:T(8,128)S(1)} %get-tuple-element.267), kind=kLoop, calls=%fused_computation.77 | loop fusion | flops 2752512 | bytes 1769504 | tf_op jit(solution)/shard_map/while/body/eval_jaxpr/jit(_where)/select_n | solution.py:33
  21.4 6.6 %fusion.27 = f32[128,64,24]{1,2,0:T(8,128)S(1)} fusion(f32[128,128,8]{1,2,0:T(8,128)S(1)} %get-tuple-element.270, f32[128,128,8]{1,2,0:T(8,128)S(1)} %get-tuple-element.271, f32[128,128,8]{1,2,0:T(8,128)S(1)} %get-tuple-element.269, f32[128,128,3]{1,2,0:T(4,128)S(1)} %copy.38), kind=kOutput, calls=%fused_computation.40 | convolution fusion | flops 303431680 | bytes 2555904 | tf_op jit(solution)/shard_map/while/body/eval_jaxpr/knm,knq->kmq/dot_general | solution.py:55
  32.1 5.8 %all-to-all-start.1 = ((f32[32,8,1536]{2,1,0:T(8,128)}), f32[32,8,1536]{2,1,0:T(8,128)S(1)}, u32[]{:S(2)}, u32[]{:S(2)}) async-start(f32[32,8,1536]{2,1,0:T(8,128)} %bitcast.27), calls=%async_computation.1 | async-start | bytes 3145728 | tf_op jit(solution)/shard_map/all_to_all | solution.py:178
  38.6 5.2 %collective-permute-start = (f32[3,1,32,128]{3,2,1,0:T(8,128)}, f32[3,1,32,128]{3,2,1,0:T(8,128)}, u32[]{:S(2)}, u32[]{:S(2)}) collective-permute-start(f32[3,1,32,128]{3,2,1,0:T(8,128)} %get-tuple-element.257), channel_id=1, source_target_pairs={{1,0},{2,1},{3,2},{4,3},{5,4},{6,5},{7,6},{8,7},{9,8},{10,9},{11,1... | collective-permute-start | bytes 147464 | tf_op jit(solution)/shard_map/ppermute | solution.py:25
  48.0 27.7 %all-to-all-done.1 = f32[32,8,1536]{2,1,0:T(8,128)S(1)} async-done(((f32[32,8,1536]{2,1,0:T(8,128)}), f32[32,8,1536]{2,1,0:T(8,128)S(1)}, u32[]{:S(2)}, u32[]{:S(2)}) %all-to-all-start.1) | async-done | bytes 1572896 | tf_op jit(solution)/shard_map/all_to_all | solution.py:178
  75.6 15.4 %reshape.228 = f32[8,32,3,8,8,8]{5,4,3,2,1,0:T(8,128)} reshape(f32[32,8,1536]{2,1,0:T(8,128)S(1)} %all-to-all-done.1) | data formatting | bytes 3145728 | tf_op jit(solution)/shard_map/reshape | solution.py:95
  91.0 47.8 %while.36 = (s32[]{:T(128)}, f32[3,8,32,128]{3,2,0,1:T(8,128)S(1)}, s32[8,32,2]{1,2,0:T(2,128)}, f32[8,32,3,8,8,8]{5,4,3,2,1,0:T(8,128)}, s32[]{:T(128)}, /*index=5*/s32[]{:T(128)}) while((s32[]{:T(128)}, f32[3,8,32,128]{3,2,0,1:T(8,128)S(1)}, s32[8,32,2]{1,2,0:T(2,128)}, f32[8,32,3,8,8,8]{5,4,3,2,1,0:T(8,128)}, s32[]{:T(128)}, ...), condition=%wide.region_5.6_spmd.clone, body=%wide.region_4.5_spmd.clone.sunk | while | flops 377725504 | bytes 11016019 | solution.py:110
  91.9 3.7 %fusion.103 = f32[32,128,3,8,8]{1,4,3,2,0:T(8,128)S(1)} fusion(f32[8,32,3,8,8,8]{5,4,3,2,1,0:T(8,128)} %get-tuple-element.353, s32[]{:T(128)} %get-tuple-element.344, s32[32,8]{1,0:T(8,128)S(1)} %get-tuple-element.336), kind=kOutput, calls=%fused_computation.22.clone.1 | convolution fusion | flops 75530240 | bytes 6292992 | tf_op jit(solution)/shard_map/while/body/eval_jaxpr/kcaij,kjz->kicaz/dot_general | solution.py:101
  97.8 3.7 %fusion.103 = f32[32,128,3,8,8]{1,4,3,2,0:T(8,128)S(1)} fusion(f32[8,32,3,8,8,8]{5,4,3,2,1,0:T(8,128)} %get-tuple-element.353, s32[]{:T(128)} %get-tuple-element.344, s32[32,8]{1,0:T(8,128)S(1)} %get-tuple-element.336), kind=kOutput, calls=%fused_computation.22.clone.1 | convolution fusion | flops 75530240 | bytes 6292992 | tf_op jit(solution)/shard_map/while/body/eval_jaxpr/kcaij,kjz->kicaz/dot_general | solution.py:101
  103.8 3.7 %fusion.103 = f32[32,128,3,8,8]{1,4,3,2,0:T(8,128)S(1)} fusion(f32[8,32,3,8,8,8]{5,4,3,2,1,0:T(8,128)} %get-tuple-element.353, s32[]{:T(128)} %get-tuple-element.344, s32[32,8]{1,0:T(8,128)S(1)} %get-tuple-element.336), kind=kOutput, calls=%fused_computation.22.clone.1 | convolution fusion | flops 75530240 | bytes 6292992 | tf_op jit(solution)/shard_map/while/body/eval_jaxpr/kcaij,kjz->kicaz/dot_general | solution.py:101
  109.8 3.7 %fusion.103 = f32[32,128,3,8,8]{1,4,3,2,0:T(8,128)S(1)} fusion(f32[8,32,3,8,8,8]{5,4,3,2,1,0:T(8,128)} %get-tuple-element.353, s32[]{:T(128)} %get-tuple-element.344, s32[32,8]{1,0:T(8,128)S(1)} %get-tuple-element.336), kind=kOutput, calls=%fused_computation.22.clone.1 | convolution fusion | flops 75530240 | bytes 6292992 | tf_op jit(solution)/shard_map/while/body/eval_jaxpr/kcaij,kjz->kicaz/dot_general | solution.py:101
  115.7 3.7 %fusion.103 = f32[32,128,3,8,8]{1,4,3,2,0:T(8,128)S(1)} fusion(f32[8,32,3,8,8,8]{5,4,3,2,1,0:T(8,128)} %get-tuple-element.353, s32[]{:T(128)} %get-tuple-element.344, s32[32,8]{1,0:T(8,128)S(1)} %get-tuple-element.336), kind=kOutput, calls=%fused_computation.22.clone.1 | convolution fusion | flops 75530240 | bytes 6292992 | tf_op jit(solution)/shard_map/while/body/eval_jaxpr/kcaij,kjz->kicaz/dot_general | solution.py:101
  121.6 3.7 %fusion.103 = f32[32,128,3,8,8]{1,4,3,2,0:T(8,128)S(1)} fusion(f32[8,32,3,8,8,8]{5,4,3,2,1,0:T(8,128)} %get-tuple-element.353, s32[]{:T(128)} %get-tuple-element.344, s32[32,8]{1,0:T(8,128)S(1)} %get-tuple-element.336), kind=kOutput, calls=%fused_computation.22.clone.1 | convolution fusion | flops 75530240 | bytes 6292992 | tf_op jit(solution)/shard_map/while/body/eval_jaxpr/kcaij,kjz->kicaz/dot_general | solution.py:101
  127.6 3.7 %fusion.103 = f32[32,128,3,8,8]{1,4,3,2,0:T(8,128)S(1)} fusion(f32[8,32,3,8,8,8]{5,4,3,2,1,0:T(8,128)} %get-tuple-element.353, s32[]{:T(128)} %get-tuple-element.344, s32[32,8]{1,0:T(8,128)S(1)} %get-tuple-element.336), kind=kOutput, calls=%fused_computation.22.clone.1 | convolution fusion | flops 75530240 | bytes 6292992 | tf_op jit(solution)/shard_map/while/body/eval_jaxpr/kcaij,kjz->kicaz/dot_general | solution.py:101
  133.6 3.7 %fusion.103 = f32[32,128,3,8,8]{1,4,3,2,0:T(8,128)S(1)} fusion(f32[8,32,3,8,8,8]{5,4,3,2,1,0:T(8,128)} %get-tuple-element.353, s32[]{:T(128)} %get-tuple-element.344, s32[32,8]{1,0:T(8,128)S(1)} %get-tuple-element.336), kind=kOutput, calls=%fused_computation.22.clone.1 | convolution fusion | flops 75530240 | bytes 6292992 | tf_op jit(solution)/shard_map/while/body/eval_jaxpr/kcaij,kjz->kicaz/dot_general | solution.py:101
  140.9 3.2 %collective-permute-start.2 = (f32[3,1,32,128]{3,2,1,0:T(8,128)S(1)}, f32[3,1,32,128]{3,2,1,0:T(8,128)S(1)}, u32[]{:S(2)}, u32[]{:S(2)}) collective-permute-start(f32[3,1,32,128]{3,2,1,0:T(8,128)S(1)} %get-tuple-element.244), channel_id=1, source_target_pairs={{1,0},{2,1},{3,2},{4,3},{5,4},{6,5},{7,6},{8,7},{9,8},{10,9},{11,1... | collective-permute-start | bytes 147464 | tf_op jit(solution)/shard_map/ppermute | solution.py:25
  145.8 5.4 %collective-permute-done.3 = f32[3,1,32,128]{3,2,1,0:T(8,128)S(1)} collective-permute-done((f32[3,1,32,128]{3,2,1,0:T(8,128)S(1)}, f32[3,1,32,128]{3,2,1,0:T(8,128)S(1)}, u32[]{:S(2)}, u32[]{:S(2)}) %collective-permute-start.3) | collective-permute-done | bytes 49184 | tf_op jit(solution)/shard_map/ppermute | solution.py:23
  154.0 5.4 %collective-permute-done.5 = f32[3,1,32,128]{3,2,1,0:T(8,128)S(1)} collective-permute-done((f32[3,1,32,128]{3,2,1,0:T(8,128)S(1)}, f32[3,1,32,128]{3,2,1,0:T(8,128)S(1)}, u32[]{:S(2)}, u32[]{:S(2)}) %collective-permute-start.5) | collective-permute-done | bytes 49184 | tf_op jit(solution)/shard_map/ppermute | solution.py:23
  159.9 67.0 %while.35 = (s32[]{:T(128)}, f32[8,32,1536]{2,1,0:T(8,128)}, s32[8,32,2]{1,2,0:T(2,128)}, f32[3,8,32,128]{3,2,1,0:T(8,128)S(1)}, s32[]{:T(128)}) while((s32[]{:T(128)}, f32[8,32,1536]{2,1,0:T(8,128)}, s32[8,32,2]{1,2,0:T(2,128)}, f32[3,8,32,128]{3,2,1,0:T(8,128)S(1)}, s32[]{:T(128)}) %tuple.112), condition=%wide.region_7.8_spmd, body=%wide.region_6.7_spmd.sunk | while | flops 320905792 | bytes 3348289 | solution.py:131
  197.3 2.4 copy.67
  227.6 2.7 all-to-all-start.2
  230.3 37.8 %all-to-all-done.2 = f32[32,8,1536]{2,1,0:T(8,128)S(1)} async-done(((f32[32,8,1536]{2,1,0:T(8,128)}), f32[32,8,1536]{2,1,0:T(8,128)S(1)}, u32[]{:S(2)}, u32[]{:S(2)}) %all-to-all-start.2) | async-done | bytes 1572896 | tf_op jit(solution)/shard_map/all_to_all | solution.py:184
  272.0 4.1 %fusion.36 = f32[128,128,3]{1,2,0:T(4,128)S(1)} fusion(f32[128,3,64,8]{2,3,1,0:T(8,128)S(1)} %copy.49, f32[128,128,8]{1,2,0:T(8,128)S(1)} %copy-done.5, f32[128,128,8]{1,2,0:T(8,128)S(1)} %copy-done.7, f32[128,128,8]{1,2,0:T(8,128)S(1)} %copy-done.3), kind=kOutput, calls=%fused_computation.50 | convolution fusion | flops 303775744 | bytes 2555904
  (185 shorter events, 111.1 us)
Async XLA Ops:
  5.6 25.9 %all-to-all-start = ((s32[32,8,2]{1,2,0:T(2,128)}), s32[32,8,2]{1,2,0:T(2,128)S(1)}, u32[]{:S(2)}, u32[]{:S(2)}) async-start(s32[32,8,2]{1,2,0:T(2,128)} %copy.36), calls=%async_computation | async-start | bytes 65536 | tf_op jit(solution)/shard_map/all_to_all | solution.py:179
  20.3 0.8 copy-start.2
  20.3 1.0 copy-start.4
  20.3 1.1 copy-start.6
  31.5 0.6 copy-start.12
  31.5 6.4 %copy-start = (f32[3,8,32,128]{3,2,1,0:T(8,128)S(1)}, f32[3,8,32,128]{3,2,1,0:T(8,128)}, u32[]{:S(2)}) copy-start(f32[3,8,32,128]{3,2,1,0:T(8,128)} %param.9) | copy-start | bytes 1179652
  32.1 43.5 %all-to-all-start.1 = ((f32[32,8,1536]{2,1,0:T(8,128)}), f32[32,8,1536]{2,1,0:T(8,128)S(1)}, u32[]{:S(2)}, u32[]{:S(2)}) async-start(f32[32,8,1536]{2,1,0:T(8,128)} %bitcast.27), calls=%async_computation.1 | async-start | bytes 3145728 | tf_op jit(solution)/shard_map/all_to_all | solution.py:178
  38.6 100.2 %collective-permute-start = (f32[3,1,32,128]{3,2,1,0:T(8,128)}, f32[3,1,32,128]{3,2,1,0:T(8,128)}, u32[]{:S(2)}, u32[]{:S(2)}) collective-permute-start(f32[3,1,32,128]{3,2,1,0:T(8,128)} %get-tuple-element.257), channel_id=1, source_target_pairs={{1,0},{2,1},{3,2},{4,3},{5,4},{6,5},{7,6},{8,7},{9,8},{10,9},{11,1... | collective-permute-start | bytes 147464 | tf_op jit(solution)/shard_map/ppermute | solution.py:25
  43.8 95.0 %collective-permute-start.1 = (f32[3,1,32,128]{3,2,1,0:T(8,128)}, f32[3,1,32,128]{3,2,1,0:T(8,128)}, u32[]{:S(2)}, u32[]{:S(2)}) collective-permute-start(f32[3,1,32,128]{3,2,1,0:T(8,128)} %get-tuple-element.256), channel_id=1, source_target_pairs={{0,1},{1,2},{2,3},{3,4},{4,5},{5,6},{6,7},{7,8},{8,9},{9,10},{10,1... | collective-permute-start | bytes 147464 | tf_op jit(solution)/shard_map/ppermute | solution.py:23
  45.2 2.0 copy-start.13
  91.0 47.8 %copy-start.8 = (f32[3,8,32,127]{3,2,1,0:T(8,128)S(1)}, f32[3,8,32,127]{3,2,1,0:T(8,128)}, u32[]{:S(2)}) copy-start(f32[3,8,32,127]{3,2,1,0:T(8,128)} %get-tuple-element.262) | copy-start | bytes 1170436
  91.0 47.8 %copy-start.9 = (f32[3,8,32,127]{3,2,1,0:T(8,128)S(1)}, f32[3,8,32,127]{3,2,1,0:T(8,128)}, u32[]{:S(2)}) copy-start(f32[3,8,32,127]{3,2,1,0:T(8,128)} %get-tuple-element.263) | copy-start | bytes 1170436
  91.0 47.8 %copy-start.10 = (f32[3,8,32,1]{3,2,1,0:T(8,128)S(1)}, f32[3,8,32,1]{3,2,1,0:T(8,128)}, u32[]{:S(2)}) copy-start(f32[3,8,32,1]{3,2,1,0:T(8,128)} %get-tuple-element.264) | copy-start | bytes 9220
  91.0 47.8 %copy-start.11 = (f32[3,8,32,1]{3,2,1,0:T(8,128)S(1)}, f32[3,8,32,1]{3,2,1,0:T(8,128)}, u32[]{:S(2)}) copy-start(f32[3,8,32,1]{3,2,1,0:T(8,128)} %get-tuple-element.265) | copy-start | bytes 9220
  140.9 4.9 %collective-permute-start.2 = (f32[3,1,32,128]{3,2,1,0:T(8,128)S(1)}, f32[3,1,32,128]{3,2,1,0:T(8,128)S(1)}, u32[]{:S(2)}, u32[]{:S(2)}) collective-permute-start(f32[3,1,32,128]{3,2,1,0:T(8,128)S(1)} %get-tuple-element.244), channel_id=1, source_target_pairs={{1,0},{2,1},{3,2},{4,3},{5,4},{6,5},{7,6},{8,7},{9,8},{10,9},{11,1... | collective-permute-start | bytes 147464 | tf_op jit(solution)/shard_map/ppermute | solution.py:25
  144.1 7.1 %collective-permute-start.3 = (f32[3,1,32,128]{3,2,1,0:T(8,128)S(1)}, f32[3,1,32,128]{3,2,1,0:T(8,128)S(1)}, u32[]{:S(2)}, u32[]{:S(2)}) collective-permute-start(f32[3,1,32,128]{3,2,1,0:T(8,128)S(1)} %get-tuple-element.243), channel_id=1, source_target_pairs={{0,1},{1,2},{2,3},{3,4},{4,5},{5,6},{6,7},{7,8},{8,9},{9,10},{10,1... | collective-permute-start | bytes 147464 | tf_op jit(solution)/shard_map/ppermute | solution.py:23
  152.2 1.8 collective-permute-start.4
  152.2 7.2 %collective-permute-start.5 = (f32[3,1,32,128]{3,2,1,0:T(8,128)S(1)}, f32[3,1,32,128]{3,2,1,0:T(8,128)S(1)}, u32[]{:S(2)}, u32[]{:S(2)}) collective-permute-start(f32[3,1,32,128]{3,2,1,0:T(8,128)S(1)} %get-tuple-element.230), channel_id=1, source_target_pairs={{0,1},{1,2},{2,3},{3,4},{4,5},{5,6},{6,7},{7,8},{8,9},{9,10},{10,1... | collective-permute-start | bytes 147464 | tf_op jit(solution)/shard_map/ppermute | solution.py:23
  226.8 0.7 copy-start.1
  227.6 40.5 %all-to-all-start.2 = ((f32[32,8,1536]{2,1,0:T(8,128)}), f32[32,8,1536]{2,1,0:T(8,128)S(1)}, u32[]{:S(2)}, u32[]{:S(2)}) async-start(f32[32,8,1536]{2,1,0:T(8,128)} %bitcast.153), calls=%async_computation.2 | async-start | bytes 3145728 | tf_op jit(solution)/shard_map/all_to_all | solution.py:184
  270.2 1.8 copy-start.3
  270.2 1.8 copy-start.5
  270.2 1.8 copy-start.7
where the time goes:
time: 278 us; the launch traced here: 277 us
  local copies, waits for them, and re-layouts  81.8 us (29%)
  waiting for transfers between devices  79.2 us (28%)
  matrix products  75.8 us (27%)
  starting transfers between devices  24.8 us (9%)
  other arithmetic  13.6 us (5%)
    all_to_all x1, waiting for transfers between devices, body(): lax.all_to_all(local_values, 'slab', split_axis=0, concat_axis=0, tiled=T...  37.8 us
    dot_general x8, matrix products, add_group(): jnp.einsum('kcaij,kjz->kicaz', patch_group, col_hot, precision=lax.Precis...  29.7 us
    all_to_all x1, waiting for transfers between devices, body(): lax.all_to_all(send_patches, 'slab', split_axis=0, concat_axis=0, tiled=T...  27.7 us
    transpose x8, local copies, waits for them, and re-layouts, read_group(): jnp.einsum('kiy,kcayj->kcaij', row_hot, partial_value, precision=lax.Prec...  19.4 us
    dynamic_update_slice x16, local copies, waits for them, and re-layouts, around_blocks(): result = lax.map(read_group, shaped_offsets)  16.6 us
    reshape x1, local copies, waits for them, and re-layouts, place(): shaped_flat = flat.reshape(count // group, group, 3, CX, 8, 8)  15.4 us
    dot_general x8, matrix products, read_group(): jnp.einsum('kiy,kcayj->kcaij', row_hot, partial_value, precision=lax.Prec...  13.3 us
    dot_general x8, matrix products, read_group(): jnp.einsum('cayz,kjz->kcayj', field, col_hot, precision=lax.Precision.HIG...  11.5 us
  transfers between devices with their start and end apart: 9, of which 6 were waited for; matrix products, arithmetic and copies ran while one was open for 31% of the time, Pallas kernels for 0%

commit v1 on v0

v1 whole, which is shorter than its diff:
```python
import functools

import jax
import jax.numpy as jnp
from jax import lax
from jax.experimental import pallas as pl
from jax.experimental.pallas import tpu as pltpu
from jax.sharding import PartitionSpec as P

CX = 8
SUBSTEPS = 3
TAPS = 8
NZF = 32
ROWS = 7
time_step = 0.1
viscosity = 0.2
COEF = (0.138840092, 0.00867750575, 0.000192567891, 2.21000608e-06, 1.5527319e-08, 7.70041313e-11)


def phi(r):
    u = jnp.maximum(4.0 - r * r, 0.0)
    q = jnp.full_like(u, COEF[-1])
    for c in COEF[-2::-1]:
        q = q * u + c
    q = q * u
    return q * q


def split(x):
    high = x.astype(jnp.bfloat16)
    return high, (x - high.astype(jnp.float32)).astype(jnp.bfloat16)


def joint_weights(rec, s, r, cap, start, iota8):
    cx = rec[s, r:r + 1, :]
    cy = rec[s, cap + r:cap + r + 1, :]
    first = rec[s, 6 * cap + r:6 * cap + r + 1, 0:1]
    wx = phi(iota8 - 1.0 - (CX - 4) * cx)
    wy = phi(iota8 + (start.astype(jnp.float32) - first) - 5.0 * cy)
    return (wy[:, None, :] * wx[None, :, :]).reshape(TAPS * CX, cx.shape[-1])


def z_weights(rec, s, r, cap, iota32):
    cz = rec[s, 2 * cap + r:2 * cap + r + 1, :]
    first = rec[s, 6 * cap + r:6 * cap + r + 1, 1:2]
    return phi(iota32 - first - 5.0 * cz)


def window_start(starts, slot, ny):
    return jnp.clip(starts[slot] - 1, 0, ny - TAPS)


def pack_kernel(cap, slab, offset, coords, force, send, slots, count):
    devices = send.shape[0]
    send[...] = jnp.zeros_like(send)

    def clear(d, carry):
        count[d] = 0
        return carry

    lax.fori_loop(0, devices, clear, 0)
    lane = lax.broadcasted_iota(jnp.int32, (1, send.shape[2]), 1)

    def one(k, carry):
        d = slab[k]
        r = count[d]
        count[d] = r + 1
        slots[k] = d * cap + r
        for c in range(3):
            send[d, pl.ds(c * cap + r, 1), :] = coords[k, c:c + 1, :]
            send[d, pl.ds((3 + c) * cap + r, 1), :] = force[k, c:c + 1, :]
        oy = offset[2 * k].astype(jnp.float32)
        oz = offset[2 * k + 1].astype(jnp.float32)
        send[d, pl.ds(6 * cap + r, 1), :] = jnp.where(lane == 0, oy, oz)
        return carry

    lax.fori_loop(0, coords.shape[0], one, 0, unroll=4)


def spread_kernel(cap, ny, starts, rec, out, acc):
    nodes = rec.shape[2]
    acc[...] = jnp.zeros_like(acc)
    iota8 = lax.broadcasted_iota(jnp.int32, (TAPS, nodes), 0).astype(jnp.float32)
    iota32 = lax.broadcasted_iota(jnp.int32, (NZF, nodes), 0).astype(jnp.float32)

    def source(s, carry):
        for r in range(cap):
            start = window_start(starts, s * cap + r, ny)
            joint = joint_weights(rec, s, r, cap, start, iota8)
            wz = z_weights(rec, s, r, cap, iota32)
            fz = jnp.concatenate(
                [rec[s, (3 + c) * cap + r:(3 + c) * cap + r + 1, :] * wz for c in range(3)], axis=0
            )
            jh, jl = split(joint)
            fh, fl = split(fz)
            patch = lax.dot_general(
                jnp.concatenate([jh, jl, jh], axis=1),
                jnp.concatenate([fh, fh, fl], axis=1),
                (((1,), (1,)), ((), ())),
                preferred_element_type=jnp.float32,
            )
            rows = pl.ds(pl.multiple_of(start * CX, CX), TAPS * CX)
            acc[rows, 0:3 * NZF] += patch
        return carry

    lax.fori_loop(0, rec.shape[0], source, 0)
    for a in range(CX):
        out[a] = acc[pl.ds(a, ny, stride=CX), :]


def fluid_kernel(cap, starts, vel, vleft, vright, fmid, fleft, fright, rec, new, back, u0, u1, fext, u4):
    planes, ny, nz = vel.shape[1], vel.shape[2], vel.shape[3]
    nodes = rec.shape[2]
    u0[:, 0:3] = vleft[...]
    u0[:, 3:3 + planes] = vel[...]
    u0[:, 3 + planes:6 + planes] = vright[...]
    fext[0:2] = fleft[...]
    fext[2:2 + planes] = fmid[...]
    fext[2 + planes:4 + planes] = fright[...]
    lane = lax.broadcasted_iota(jnp.int32, (ny, nz), 1)

    def step(src, dst, first, last):
        def plane(p, carry):
            packed = fext[p - 1]
            center = [src[c, p] for c in range(3)]
            for c in range(3):
                mid = center[c]
                ahead = src[c, p + 1]
                behind = src[c, p - 1]
                y_plus = pltpu.roll(mid, ny - 1, 0)
                y_minus = pltpu.roll(mid, 1, 0)
                z_plus = pltpu.roll(mid, nz - 1, 1)
                z_minus = pltpu.roll(mid, 1, 1)
                push = packed if c == 0 else pltpu.roll(packed, nz - c * NZF, 1)
                push = jnp.where(lane < NZF, push, 0.0)
                laplace = ahead + behind + y_plus + y_minus + z_plus + z_minus - 6.0 * mid
                advect = (
                    center[0] * (ahead - behind)
                    + center[1] * (y_plus - y_minus)
                    + center[2] * (z_plus - z_minus)
                ) * 0.5
                dst[c, p] = mid + time_step * (viscosity * laplace - advect + push)
            return carry

        lax.fori_loop(first, last, plane, 0)

    step(u0, u1, 1, planes + 5)
    step(u1, u0, 2, planes + 4)
    step(u0, u1, 3, planes + 3)
    new[...] = u1[:, 3:3 + planes]

    def gather(a, carry):
        for c in range(3):
            u = u1[c, 3 + a][:, 0:NZF]
            high = u.astype(jnp.bfloat16).astype(jnp.float32)
            low = u - high
            u4[c, pl.ds(a, ny, stride=CX), :] = jnp.concatenate([high, low, high, low], axis=1)
        return carry

    for a in range(CX):
        gather(a, 0)

    iota8 = lax.broadcasted_iota(jnp.int32, (TAPS, nodes), 0).astype(jnp.float32)
    iota32 = lax.broadcasted_iota(jnp.int32, (NZF, nodes), 0).astype(jnp.float32)

    def source(s, carry):
        for r in range(cap):
            start = window_start(starts, s * cap + r, ny)
            joint = joint_weights(rec, s, r, cap, start, iota8)
            wh, wl = split(z_weights(rec, s, r, cap, iota32))
            rows = pl.ds(pl.multiple_of(start * CX, CX), TAPS * CX)
            window = jnp.concatenate([u4[c, rows, :] for c in range(3)], axis=0).astype(jnp.bfloat16)
            part = jnp.dot(
                window, jnp.concatenate([wh, wh, wl, wl], axis=0), preferred_element_type=jnp.float32
            )
            for c in range(3):
                mine = part[c * TAPS * CX:(c + 1) * TAPS * CX] * joint
                back[s, c * cap + r:c * cap + r + 1, :] = jnp.sum(mine, axis=0, keepdims=True)
        return carry

    lax.fori_loop(0, rec.shape[0], source, 0)


def unpack_kernel(cap, slots, got, out):
    def one(k, carry):
        slot = slots[k]
        d = slot // cap
        r = slot - d * cap
        for c in range(3):
            out[k, c:c + 1, :] = got[d, pl.ds(c * cap + r, 1), :]
        return carry

    lax.fori_loop(0, out.shape[0], one, 0, unroll=4)


VMEM = pl.BlockSpec(memory_space=pltpu.VMEM)
SMEM = pl.BlockSpec(memory_space=pltpu.SMEM)
PARAMS = pltpu.CompilerParams(vmem_limit_bytes=40 * 1024 * 1024)


def body(velocity, node_coords, node_force, block_slab, block_offset):
    devices = lax.axis_size("slab")
    blocks, _, nodes = node_coords.shape
    cap = 2 * blocks // devices
    _, planes, ny, nz = velocity.shape
    f32 = jnp.float32

    up = [(i, (i + 1) % devices) for i in range(devices)]
    down = [((i + 1) % devices, i) for i in range(devices)]
    vleft = lax.ppermute(velocity[:, planes - 3:], "slab", up)
    vright = lax.ppermute(velocity[:, :3], "slab", down)

    send, slots = pl.pallas_call(
        functools.partial(pack_kernel, cap),
        out_shape=(
            jax.ShapeDtypeStruct((devices, ROWS * cap, nodes), f32),
            jax.ShapeDtypeStruct((blocks,), jnp.int32),
        ),
        in_specs=[SMEM, SMEM, VMEM, VMEM],
        out_specs=(VMEM, SMEM),
        scratch_shapes=[pltpu.SMEM((devices,), jnp.int32)],
        compiler_params=PARAMS,
    )(block_slab.reshape(blocks), block_offset.reshape(2 * blocks), node_coords, node_force)

    rec = lax.all_to_all(send, "slab", split_axis=0, concat_axis=0, tiled=True)
    starts = rec[:, 6 * cap:, 0].astype(jnp.int32).reshape(devices * cap)

    fmid = pl.pallas_call(
        functools.partial(spread_kernel, cap, ny),
        out_shape=jax.ShapeDtypeStruct((planes, ny, nz), f32),
        in_specs=[SMEM, VMEM],
        out_specs=VMEM,
        scratch_shapes=[pltpu.VMEM((ny * CX, nz), f32)],
        compiler_params=PARAMS,
    )(starts, rec)

    fleft = lax.ppermute(fmid[planes - 2:], "slab", up)
    fright = lax.ppermute(fmid[:2], "slab", down)

    new, back = pl.pallas_call(
        functools.partial(fluid_kernel, cap),
        out_shape=(
            jax.ShapeDtypeStruct(velocity.shape, f32),
            jax.ShapeDtypeStruct((devices, 3 * cap, nodes), f32),
        ),
        in_specs=[SMEM] + [VMEM] * 7,
        out_specs=(VMEM, VMEM),
        scratch_shapes=[
            pltpu.VMEM((3, planes + 6, ny, nz), f32),
            pltpu.VMEM((3, planes + 6, ny, nz), f32),
            pltpu.VMEM((planes + 4, ny, nz), f32),
            pltpu.VMEM((3, ny * CX, nz), f32),
        ],
        compiler_params=PARAMS,
    )(starts, velocity, vleft, vright, fmid, fleft, fright, rec)

    got = lax.all_to_all(back, "slab", split_axis=0, concat_axis=0, tiled=True)

    node_velocity = pl.pallas_call(
        functools.partial(unpack_kernel, cap),
        out_shape=jax.ShapeDtypeStruct((blocks, 3, nodes), f32),
        in_specs=[SMEM, VMEM],
        out_specs=VMEM,
        compiler_params=PARAMS,
    )(slots, got)
    return new, node_velocity


def solution(mesh):
    return jax.shard_map(
        body,
        mesh=mesh,
        in_specs=(
            P(None, "slab", None, None),
            P("slab", None, None),
            P("slab", None, None),
            P("slab", None),
            P("slab", None),
        ),
        out_specs=(P(None, "slab", None, None), P("slab", None, None)),
        check_vma=False,
    )
```

time: 278 us -> 100 us (0.36)
  local copies, waits for them, and re-layouts: 81.8 us -> 3.64 us
  matrix products: 75.8 us -> 0 us
  waiting for transfers between devices: 79.2 us -> 25.8 us
  Pallas kernels: 0 us -> 39.4 us
  blocking collectives: 0 us -> 14.9 us
  other arithmetic: 13.6 us -> 0.61 us
  starting transfers between devices: 24.8 us -> 14.7 us
    dot_general x33 -> x0, matrix products: 71.7 us -> none  [the longest x8 29.7 us: add_group(): jnp.einsum('kcaij,kjz->kicaz', patch_group, col_hot, precision=lax.Precis...]
    all_to_all x3 -> x1, waiting for transfers between devices: 65.5 us -> 18.9 us  [body(): rec = lax.all_to_all(send, 'slab', split_axis=0, concat_axis=0, tiled=True)]
    pallas_call x0 -> x4, Pallas kernels: none -> 39.4 us  [the longest x1 17.9 us: body(): pl.pallas_call(functools.partial(spread_kernel, cap, ny), out_shape=jax.S...]
    transpose x10 -> x0, local copies, waits for them, and re-layouts: 20.6 us -> none  [the longest x8 19.4 us: read_group(): jnp.einsum('kiy,kcayj->kcaij', row_hot, partial_value, precision=lax.Prec...]
    reshape x4 -> x1, local copies, waits for them, and re-layouts: 17.5 us -> 0.14 us  [body(): block_offset.reshape(2 * blocks)]
    dynamic_update_slice x16 -> x0, local copies, waits for them, and re-layouts: 16.6 us -> none  [around_blocks(): result = lax.map(read_group, shaped_offsets)]
    all_to_all x0 -> x1, blocking collectives: none -> 14.9 us  [body(): got = lax.all_to_all(back, 'slab', split_axis=0, concat_axis=0, tiled=True)]
    squeeze x16 -> x0, local copies, waits for them, and re-layouts: 10.6 us -> none  [place(): total, unused = lax.scan(add_group, start, (shaped_flat, shaped_offsets))]
  transfers between devices with their start and end apart: 9 -> 5, of which waited for: 6 -> 3; matrix products, arithmetic and copies ran while one was open for 31% -> 1% of each run, Pallas kernels for 0% -> 18%
where the time goes in v1:
time: 100 us; the launch traced here: 99.9 us
  Pallas kernels  39.4 us (39%)
  waiting for transfers between devices  25.8 us (26%)
  blocking collectives  14.9 us (15%)
  starting transfers between devices  14.7 us (15%)
  local copies, waits for them, and re-layouts  3.64 us (4%)
    all_to_all x1, waiting for transfers between devices, body(): rec = lax.all_to_all(send, 'slab', split_axis=0, concat_axis=0, tiled=True)  18.9 us
    pallas_call x1, Pallas kernels, body(): pl.pallas_call(functools.partial(spread_kernel, cap, ny), out_shape=jax.S...  17.9 us
    pallas_call x1, Pallas kernels, body(): pl.pallas_call(functools.partial(fluid_kernel, cap), out_shape=(jax.Shape...  17.4 us
    all_to_all x1, blocking collectives, body(): got = lax.all_to_all(back, 'slab', split_axis=0, concat_axis=0, tiled=True)  14.9 us
    all_to_all x1, starting transfers between devices, body(): rec = lax.all_to_all(send, 'slab', split_axis=0, concat_axis=0, tiled=True)  7.3 us
    ppermute x1, waiting for transfers between devices, body(): fleft = lax.ppermute(fmid[planes - 2:], 'slab', up)  5.34 us
    ppermute x1, starting transfers between devices, body(): vright = lax.ppermute(velocity[:, :3], 'slab', down)  5.27 us
    unnamed x10, local copies, waits for them, and re-layouts  3.38 us
  transfers between devices with their start and end apart: 5, of which 3 were waited for; matrix products, arithmetic and copies ran while one was open for 1% of the time, Pallas kernels for 18%

profile of v1, /device:TPU:0, one launch (start us, length us, event | category | flops | bytes accessed | tf_op | source)
XLA Modules:
  0.0 99.9 jit_solution(5507681372323874484)
XLA Ops:
  0.6 0.8 copy.10
  1.4 0.1 reshape.14.offset
  1.6 0.0 copy-start.2
  1.6 1.1 %copy.11.coords = f32[128,3,128]{2,1,0:T(4,128)S(1)} copy(f32[128,3,128]{2,0,1:T(8,128)} %param.6) | data formatting | bytes 393216 | tf_op args[1]
  2.7 0.1 copy.12.force
  2.8 0.0 copy-start.1
  2.8 0.6 copy-done.1
  3.5 2.6 %shard_map.68 = (f32[32,56,128]{2,1,0:T(8,128)}, s32[128]{0:T(128)S(1)}) custom-call(s32[128]{0:T(128)S(1)} %bitcast.1, s32[256]{0:T(256)S(1)} %reshape.14.offset, f32[128,3,128]{2,1,0:T(4,128)S(1)} %copy.11.coords, f32[128,3,128]{2,1,0:T(4,128)S(1)} %copy.12.force), custom_call_target="tpu_custom_call" | custom-call | tf_op jit(solution)/shard_map/pallas_call | solution.py:213
  6.1 0.0 copy-start
  6.1 7.3 %all-to-all-start = ((f32[32,56,128]{2,1,0:T(8,128)}), f32[32,56,128]{2,1,0:T(8,128)S(1)}, u32[]{:S(2)}, u32[]{:S(2)}) async-start(f32[32,56,128]{2,1,0:T(8,128)} %get-tuple-element.6), calls=%async_computation | async-start | bytes 1835008 | tf_op jit(solution)/shard_map/all_to_all | solution.py:225
  13.5 5.3 %collective-permute-start.1 = (f32[3,3,32,128]{3,2,1,0:T(8,128)S(1)}, f32[3,3,32,128]{3,2,1,0:T(8,128)S(1)}, u32[]{:S(2)}, u32[]{:S(2)}) collective-permute-start(f32[3,3,32,128]{3,2,1,0:T(8,128)S(1)} %get-tuple-element.14), channel_id=1, source_target_pairs={{1,0},{2,1},{3,2},{4,3},{5,4},{6,5},{7,6},{8,7},{9,8},{10,9},{11,1... | collective-permute-start | bytes 442376 | tf_op jit(solution)/shard_map/ppermute | solution.py:211
  18.8 0.0 collective-permute-start
  18.8 18.9 %all-to-all-done.rec = f32[32,56,128]{2,1,0:T(8,128)S(1)} async-done(((f32[32,56,128]{2,1,0:T(8,128)}), f32[32,56,128]{2,1,0:T(8,128)S(1)}, u32[]{:S(2)}, u32[]{:S(2)}) %all-to-all-start) | async-done | bytes 917536 | tf_op jit(solution)/shard_map/all_to_all | solution.py:225
  37.7 0.6 fusion
  38.3 0.1 convert_element_type.8.starts
  38.4 17.9 %shard_map.69.fmid = f32[8,32,128]{2,1,0:T(8,128)S(1)} custom-call(s32[256]{0:T(256)S(1)} %convert_element_type.8.starts, f32[32,56,128]{2,1,0:T(8,128)S(1)} %all-to-all-done.rec), custom_call_target="tpu_custom_call" | custom-call | tf_op jit(solution)/shard_map/pallas_call | solution.py:228
  56.3 2.2 %collective-permute-start.3 = (f32[2,32,128]{2,1,0:T(8,128)S(1)}, f32[2,32,128]{2,1,0:T(8,128)S(1)}, u32[]{:S(2)}, u32[]{:S(2)}) collective-permute-start(f32[2,32,128]{2,1,0:T(8,128)S(1)} %get-tuple-element.16), channel_id=1, source_target_pairs={{1,0},{2,1},{3,2},{4,3},{5,4},{6,5},{7,6},{8,7},{9,8},{10,9},{11,1... | collective-permute-start | bytes 98312 | tf_op jit(solution)/shard_map/ppermute | solution.py:238
  58.4 0.0 collective-permute-start.2
  58.5 1.6 %collective-permute-done.3.fright = f32[2,32,128]{2,1,0:T(8,128)S(1)} collective-permute-done((f32[2,32,128]{2,1,0:T(8,128)S(1)}, f32[2,32,128]{2,1,0:T(8,128)S(1)}, u32[]{:S(2)}, u32[]{:S(2)}) %collective-permute-start.3) | collective-permute-done | bytes 32800 | tf_op jit(solution)/shard_map/ppermute | solution.py:238
  60.0 5.3 %collective-permute-done.2.fleft = f32[2,32,128]{2,1,0:T(8,128)S(1)} collective-permute-done((f32[2,32,128]{2,1,0:T(8,128)S(1)}, f32[2,32,128]{2,1,0:T(8,128)S(1)}, u32[]{:S(2)}, u32[]{:S(2)}) %collective-permute-start.2) | collective-permute-done | bytes 32800 | tf_op jit(solution)/shard_map/ppermute | solution.py:237
  65.4 17.4 %shard_map.70 = (f32[3,8,32,128]{3,2,1,0:T(8,128)}, f32[32,24,128]{2,1,0:T(8,128)S(1)}) custom-call(s32[256]{0:T(256)S(1)} %convert_element_type.8.starts, f32[3,8,32,128]{3,2,1,0:T(8,128)S(1)} %copy-done, f32[3,3,32,128]{3,2,1,0:T(8,128)S(1)} %collective-permute-done.vleft, f32[3,3,32,128]{3,2,1,0:T(8,128)S(1)} %collective-permute-done.1.vright, ...), custom_call_target="tpu_custom_call" | custom-call | tf_op jit(solution)/shard_map/pallas_call | solution.py:240
  82.8 14.9 %all_to_all.10.got = f32[32,24,128]{2,1,0:T(8,128)S(1)} all-to-all(f32[32,24,128]{2,1,0:T(8,128)S(1)} %get-tuple-element.9), channel_id=1, replica_groups=mesh['slab'=32] {'slab'}, dimensions={0} | all-to-all | bytes 786432 | tf_op jit(solution)/shard_map/all_to_all | solution.py:257
  97.7 1.5 %shard_map.71 = f32[128,3,128]{2,1,0:T(4,128)S(1)} custom-call(s32[128]{0:T(128)S(1)} %get-tuple-element.8.slots, f32[32,24,128]{2,1,0:T(8,128)S(1)} %all_to_all.10.got), custom_call_target="tpu_custom_call" | custom-call | tf_op jit(solution)/shard_map/pallas_call | solution.py:259
  99.2 0.7 copy.13
  (6 shorter events, 0.0 us)
Async XLA Ops:
  1.6 1.1 %copy-start.2 = (f32[128,3,128]{2,0,1:T(8,128)S(1)}, f32[128,3,128]{2,0,1:T(8,128)}, u32[]{:S(2)}) copy-start(f32[128,3,128]{2,0,1:T(8,128)} %param.7) | copy-start | bytes 589828
  2.8 0.7 copy-start.1
  6.1 7.3 %copy-start = (f32[3,8,32,128]{3,2,1,0:T(8,128)S(1)}, f32[3,8,32,128]{3,2,1,0:T(8,128)}, u32[]{:S(2)}) copy-start(f32[3,8,32,128]{3,2,1,0:T(8,128)} %vel.1) | copy-start | bytes 1179652
  6.1 31.5 %all-to-all-start = ((f32[32,56,128]{2,1,0:T(8,128)}), f32[32,56,128]{2,1,0:T(8,128)S(1)}, u32[]{:S(2)}, u32[]{:S(2)}) async-start(f32[32,56,128]{2,1,0:T(8,128)} %get-tuple-element.6), calls=%async_computation | async-start | bytes 1835008 | tf_op jit(solution)/shard_map/all_to_all | solution.py:225
  13.5 45.0 %collective-permute-start.1 = (f32[3,3,32,128]{3,2,1,0:T(8,128)S(1)}, f32[3,3,32,128]{3,2,1,0:T(8,128)S(1)}, u32[]{:S(2)}, u32[]{:S(2)}) collective-permute-start(f32[3,3,32,128]{3,2,1,0:T(8,128)S(1)} %get-tuple-element.14), channel_id=1, source_target_pairs={{1,0},{2,1},{3,2},{4,3},{5,4},{6,5},{7,6},{8,7},{9,8},{10,9},{11,1... | collective-permute-start | bytes 442376 | tf_op jit(solution)/shard_map/ppermute | solution.py:211
  18.8 39.7 %collective-permute-start = (f32[3,3,32,128]{3,2,1,0:T(8,128)S(1)}, f32[3,3,32,128]{3,2,1,0:T(8,128)S(1)}, u32[]{:S(2)}, u32[]{:S(2)}) collective-permute-start(f32[3,3,32,128]{3,2,1,0:T(8,128)S(1)} %get-tuple-element.15), channel_id=1, source_target_pairs={{0,1},{1,2},{2,3},{3,4},{4,5},{5,6},{6,7},{7,8},{8,9},{9,10},{10,1... | collective-permute-start | bytes 442376 | tf_op jit(solution)/shard_map/ppermute | solution.py:210
  56.3 3.8 %collective-permute-start.3 = (f32[2,32,128]{2,1,0:T(8,128)S(1)}, f32[2,32,128]{2,1,0:T(8,128)S(1)}, u32[]{:S(2)}, u32[]{:S(2)}) collective-permute-start(f32[2,32,128]{2,1,0:T(8,128)S(1)} %get-tuple-element.16), channel_id=1, source_target_pairs={{1,0},{2,1},{3,2},{4,3},{5,4},{6,5},{7,6},{8,7},{9,8},{10,9},{11,1... | collective-permute-start | bytes 98312 | tf_op jit(solution)/shard_map/ppermute | solution.py:238
  58.4 6.9 %collective-permute-start.2 = (f32[2,32,128]{2,1,0:T(8,128)S(1)}, f32[2,32,128]{2,1,0:T(8,128)S(1)}, u32[]{:S(2)}, u32[]{:S(2)}) collective-permute-start(f32[2,32,128]{2,1,0:T(8,128)S(1)} %get-tuple-element.17), channel_id=1, source_target_pairs={{0,1},{1,2},{2,3},{3,4},{4,5},{5,6},{6,7},{7,8},{8,9},{9,10},{10,1... | collective-permute-start | bytes 98312 | tf_op jit(solution)/shard_map/ppermute | solution.py:237

commit v2 on v1

--- a/solution.py
+++ b/solution.py
@@ -44,10 +44,6 @@
     cz = rec[s, 2 * cap + r:2 * cap + r + 1, :]
     first = rec[s, 6 * cap + r:6 * cap + r + 1, 1:2]
     return phi(iota32 - first - 5.0 * cz)
-
-
-def window_start(starts, slot, ny):
-    return jnp.clip(starts[slot] - 1, 0, ny - TAPS)
 
 
 def pack_kernel(cap, slab, offset, coords, force, send, slots, count):
@@ -85,7 +81,7 @@
 
     def source(s, carry):
         for r in range(cap):
-            start = window_start(starts, s * cap + r, ny)
+            start = starts[s * cap + r]
             joint = joint_weights(rec, s, r, cap, start, iota8)
             wz = z_weights(rec, s, r, cap, iota32)
             fz = jnp.concatenate(
@@ -108,20 +104,99 @@
         out[a] = acc[pl.ds(a, ny, stride=CX), :]
 
 
-def fluid_kernel(cap, starts, vel, vleft, vright, fmid, fleft, fright, rec, new, back, u0, u1, fext, u4):
+def partner(j, n):
+    half = (j + 1) // 2
+    return n // 2 + half * (1 - 2 * (j % 2))
+
+
+def meet_all(n, me):
+    barrier = pltpu.get_barrier_semaphore()
+
+    def greet(i, carry):
+        pl.semaphore_signal(barrier, inc=1, device_id=(lax.rem(me + i, n),), device_id_type=MESH)
+        return carry
+
+    lax.fori_loop(1, n, greet, 0)
+    pl.semaphore_wait(barrier, n - 1)
+
+
+def exchange_kernel(n, send, vel, rec, vleft, vright, send_sem, recv_sem, own_sem, halo_send, halo_recv):
+    me = lax.axis_index("slab")
+    right, left = lax.rem(me + 1, n), lax.rem(me + n - 1, n)
+    planes = vel.shape[1]
+    own = pltpu.make_async_copy(send.at[me], rec.at[me], own_sem)
+    own.start()
+    meet_all(n, me)
+
+    def copy_to(i):
+        to = lax.rem(me + i, n)
+        return pltpu.make_async_remote_copy(
+            src_ref=send.at[to], dst_ref=rec.at[me], send_sem=send_sem.at[i], recv_sem=recv_sem.at[i],
+            device_id=(to,), device_id_type=MESH,
+        )
+
+    halos = [
+        pltpu.make_async_remote_copy(
+            src_ref=vel.at[:, planes - 3:], dst_ref=vleft, send_sem=halo_send.at[0], recv_sem=halo_recv.at[0],
+            device_id=(right,), device_id_type=MESH,
+        ),
+        pltpu.make_async_remote_copy(
+            src_ref=vel.at[:, 0:3], dst_ref=vright, send_sem=halo_send.at[1], recv_sem=halo_recv.at[1],
+            device_id=(left,), device_id_type=MESH,
+        ),
+    ]
+
+    def start(j, carry):
+        copy_to(partner(j, n)).start()
+        return carry
+
+    lax.fori_loop(0, n - 1, start, 0)
+    for halo in halos:
+        halo.start()
+
+    def finish(i, carry):
+        copy = pltpu.make_async_remote_copy(
+            src_ref=send.at[lax.rem(me + i, n)], dst_ref=rec.at[lax.rem(me + n - i, n)],
+            send_sem=send_sem.at[i], recv_sem=recv_sem.at[i], device_id=(right,), device_id_type=MESH,
+        )
+        copy.wait()
+        return carry
+
+    lax.fori_loop(1, n, finish, 0)
+    for halo in halos:
+        halo.wait()
+    own.wait()
+
+
+def fluid_kernel(
+    n, cap, starts, vel, vleft, vright, fmid, rec, new, got,
+    u0, u1, fext, u4, back, send_sem, recv_sem, halo_send, halo_recv,
+):
+    me = lax.axis_index("slab")
+    right, left = lax.rem(me + 1, n), lax.rem(me + n - 1, n)
     planes, ny, nz = vel.shape[1], vel.shape[2], vel.shape[3]
     nodes = rec.shape[2]
+    meet_all(n, me)
+    halos = [
+        pltpu.make_async_remote_copy(
+            src_ref=fmid.at[planes - 2:], dst_ref=fext.at[0:2], send_sem=halo_send.at[0],
+            recv_sem=halo_recv.at[0], device_id=(right,), device_id_type=MESH,
+        ),
+        pltpu.make_async_remote_copy(
+            src_ref=fmid.at[0:2], dst_ref=fext.at[2 + planes:4 + planes], send_sem=halo_send.at[1],
+            recv_sem=halo_recv.at[1], device_id=(left,), device_id_type=MESH,
+        ),
+    ]
+    for halo in halos:
+        halo.start()
     u0[:, 0:3] = vleft[...]
     u0[:, 3:3 + planes] = vel[...]
     u0[:, 3 + planes:6 + planes] = vright[...]
-    fext[0:2] = fleft[...]
-    fext[2:2 + planes] = fmid[...]
-    fext[2 + planes:4 + planes] = fright[...]
     lane = lax.broadcasted_iota(jnp.int32, (ny, nz), 1)
 
-    def step(src, dst, first, last):
+    def step(src, dst, first, last, force, shift):
         def plane(p, carry):
-            packed = fext[p - 1]
+            packed = force[p - shift]
             center = [src[c, p] for c in range(3)]
             for c in range(3):
                 mid = center[c]
@@ -144,41 +219,63 @@
 
         lax.fori_loop(first, last, plane, 0)
 
-    step(u0, u1, 1, planes + 5)
-    step(u1, u0, 2, planes + 4)
-    step(u0, u1, 3, planes + 3)
+    step(u0, u1, 3, planes + 3, fmid, 3)
+    for halo in halos:
+        halo.wait()
+    step(u0, u1, 1, 3, fext, 1)
+    step(u0, u1, planes + 3, planes + 5, fext, 1)
+    step(u1, u0, 2, 3, fext, 1)
+    step(u1, u0, 3, planes + 3, fmid, 3)
+    step(u1, u0, planes + 3, planes + 4, fext, 1)
+    step(u0, u1, 3, planes + 3, fmid, 3)
     new[...] = u1[:, 3:3 + planes]
 
-    def gather(a, carry):
+    for a in range(CX):
         for c in range(3):
             u = u1[c, 3 + a][:, 0:NZF]
             high = u.astype(jnp.bfloat16).astype(jnp.float32)
             low = u - high
-            u4[c, pl.ds(a, ny, stride=CX), :] = jnp.concatenate([high, low, high, low], axis=1)
-        return carry
-
-    for a in range(CX):
-        gather(a, 0)
+            u4[c, :, a, :] = jnp.concatenate([high, low, high, low], axis=1)
 
     iota8 = lax.broadcasted_iota(jnp.int32, (TAPS, nodes), 0).astype(jnp.float32)
     iota32 = lax.broadcasted_iota(jnp.int32, (NZF, nodes), 0).astype(jnp.float32)
 
-    def source(s, carry):
+    def answer(s, put, place):
         for r in range(cap):
-            start = window_start(starts, s * cap + r, ny)
+            start = starts[s * cap + r]
             joint = joint_weights(rec, s, r, cap, start, iota8)
             wh, wl = split(z_weights(rec, s, r, cap, iota32))
-            rows = pl.ds(pl.multiple_of(start * CX, CX), TAPS * CX)
-            window = jnp.concatenate([u4[c, rows, :] for c in range(3)], axis=0).astype(jnp.bfloat16)
+            window = jnp.concatenate(
+                [u4[c, start + i] for c in range(3) for i in range(TAPS)], axis=0
+            ).astype(jnp.bfloat16)
             part = jnp.dot(
                 window, jnp.concatenate([wh, wh, wl, wl], axis=0), preferred_element_type=jnp.float32
             )
             for c in range(3):
                 mine = part[c * TAPS * CX:(c + 1) * TAPS * CX] * joint
-                back[s, c * cap + r:c * cap + r + 1, :] = jnp.sum(mine, axis=0, keepdims=True)
-        return carry
-
-    lax.fori_loop(0, rec.shape[0], source, 0)
+                put[place, c * cap + r:c * cap + r + 1, :] = jnp.sum(mine, axis=0, keepdims=True)
+
+    def serve(j, carry):
+        i = partner(j, n)
+        s = lax.rem(me + i, n)
+        answer(s, back, s)
+        pltpu.make_async_remote_copy(
+            src_ref=back.at[s], dst_ref=got.at[me], send_sem=send_sem.at[i], recv_sem=recv_sem.at[i],
+            device_id=(s,), device_id_type=MESH,
+        ).start()
+        return carry
+
+    lax.fori_loop(0, n - 1, serve, 0)
+    answer(me, got, me)
+
+    def finish(i, carry):
+        pltpu.make_async_remote_copy(
+            src_ref=back.at[lax.rem(me + i, n)], dst_ref=got.at[lax.rem(me + n - i, n)],
+            send_sem=send_sem.at[i], recv_sem=recv_sem.at[i], device_id=(right,), device_id_type=MESH,
+        ).wait()
+        return carry
+
+    lax.fori_loop(1, n, finish, 0)
 
 
 def unpack_kernel(cap, slots, got, out):
@@ -193,6 +290,7 @@
     lax.fori_loop(0, out.shape[0], one, 0, unroll=4)
 
 
+MESH = pl.DeviceIdType.MESH
 VMEM = pl.BlockSpec(memory_space=pltpu.VMEM)
 SMEM = pl.BlockSpec(memory_space=pltpu.SMEM)
 PARAMS = pltpu.CompilerParams(vmem_limit_bytes=40 * 1024 * 1024)
@@ -205,11 +303,6 @@
     _, planes, ny, nz = velocity.shape
     f32 = jnp.float32
 
-    up = [(i, (i + 1) % devices) for i in range(devices)]
-    down = [((i + 1) % devices, i) for i in range(devices)]
-    vleft = lax.ppermute(velocity[:, planes - 3:], "slab", up)
-    vright = lax.ppermute(velocity[:, :3], "slab", down)
-
     send, slots = pl.pallas_call(
         functools.partial(pack_kernel, cap),
         out_shape=(
@@ -222,8 +315,25 @@
         compiler_params=PARAMS,
     )(block_slab.reshape(blocks), block_offset.reshape(2 * blocks), node_coords, node_force)
 
-    rec = lax.all_to_all(send, "slab", split_axis=0, concat_axis=0, tiled=True)
-    starts = rec[:, 6 * cap:, 0].astype(jnp.int32).reshape(devices * cap)
+    halo = jax.ShapeDtypeStruct((3, 3, ny, nz), f32)
+    rec, vleft, vright = pl.pallas_call(
+        functools.partial(exchange_kernel, devices),
+        out_shape=(jax.ShapeDtypeStruct(send.shape, f32), halo, halo),
+        in_specs=[VMEM, VMEM],
+        out_specs=(VMEM, VMEM, VMEM),
+        scratch_shapes=[
+            pltpu.SemaphoreType.DMA((devices,)),
+            pltpu.SemaphoreType.DMA((devices,)),
+            pltpu.SemaphoreType.DMA,
+            pltpu.SemaphoreType.DMA((2,)),
+            pltpu.SemaphoreType.DMA((2,)),
+        ],
+        compiler_params=pltpu.CompilerParams(
+            vmem_limit_bytes=40 * 1024 * 1024, collective_id=0, has_side_effects=True
+        ),
+    )(send, velocity)
+    first = rec[:, 6 * cap:, 0].astype(jnp.int32).reshape(devices * cap)
+    starts = jnp.clip(first - 1, 0, ny - TAPS)
 
     fmid = pl.pallas_call(
         functools.partial(spread_kernel, cap, ny),
@@ -234,27 +344,29 @@
         compiler_params=PARAMS,
     )(starts, rec)
 
-    fleft = lax.ppermute(fmid[planes - 2:], "slab", up)
-    fright = lax.ppermute(fmid[:2], "slab", down)
-
-    new, back = pl.pallas_call(
-        functools.partial(fluid_kernel, cap),
+    new, got = pl.pallas_call(
+        functools.partial(fluid_kernel, devices, cap),
         out_shape=(
             jax.ShapeDtypeStruct(velocity.shape, f32),
             jax.ShapeDtypeStruct((devices, 3 * cap, nodes), f32),
         ),
-        in_specs=[SMEM] + [VMEM] * 7,
+        in_specs=[SMEM] + [VMEM] * 5,
         out_specs=(VMEM, VMEM),
         scratch_shapes=[
             pltpu.VMEM((3, planes + 6, ny, nz), f32),
             pltpu.VMEM((3, planes + 6, ny, nz), f32),
             pltpu.VMEM((planes + 4, ny, nz), f32),
-            pltpu.VMEM((3, ny * CX, nz), f32),
+            pltpu.VMEM((3, ny, CX, nz), f32),
+            pltpu.VMEM((devices, 3 * cap, nodes), f32),
+            pltpu.SemaphoreType.DMA((devices,)),
+            pltpu.SemaphoreType.DMA((devices,)),
+            pltpu.SemaphoreType.DMA((2,)),
+            pltpu.SemaphoreType.DMA((2,)),
         ],
-        compiler_params=PARAMS,
-    )(starts, velocity, vleft, vright, fmid, fleft, fright, rec)
-
-    got = lax.all_to_all(back, "slab", split_axis=0, concat_axis=0, tiled=True)
+        compiler_params=pltpu.CompilerParams(
+            vmem_limit_bytes=40 * 1024 * 1024, collective_id=1, has_side_effects=True
+        ),
+    )(starts, velocity, vleft, vright, fmid, rec)
 
     node_velocity = pl.pallas_call(
         functools.partial(unpack_kernel, cap),

time: 100 us -> 85.7 us (0.86)
  Pallas kernels: 39.4 us -> 80 us
  waiting for transfers between devices: 25.8 us -> 0 us
  blocking collectives: 14.9 us -> 0 us
  starting transfers between devices: 14.7 us -> 0 us
    pallas_call x1 -> x2, Pallas kernels: 17.4 us -> 58.3 us  [the longest x1 29.3 us: body(): pl.pallas_call(functools.partial(exchange_kernel, devices), out_shape=(ja...]
    all_to_all x1 -> x0, waiting for transfers between devices: 18.9 us -> none  [body(): rec = lax.all_to_all(send, 'slab', split_axis=0, concat_axis=0, tiled=True)]
    all_to_all x1 -> x0, blocking collectives: 14.9 us -> none  [body(): got = lax.all_to_all(back, 'slab', split_axis=0, concat_axis=0, tiled=True)]
    ppermute x4 -> x0, starting transfers between devices: 7.44 us -> none  [the longest x1 5.27 us: body(): vright = lax.ppermute(velocity[:, :3], 'slab', down)]
    all_to_all x1 -> x0, starting transfers between devices: 7.3 us -> none  [body(): rec = lax.all_to_all(send, 'slab', split_axis=0, concat_axis=0, tiled=True)]
    ppermute x4 -> x0, waiting for transfers between devices: 6.93 us -> none  [the longest x1 5.34 us: body(): fleft = lax.ppermute(fmid[planes - 2:], 'slab', up)]
    unnamed x10 -> x13, local copies, waits for them, and re-layouts: 3.38 us -> 3.97 us
  transfers between devices with their start and end apart: 5 -> 0, of which waited for: 3 -> 0; matrix products, arithmetic and copies ran while one was open for 1% -> 0% of each run, Pallas kernels for 18% -> 0%
where the time goes in v2:
time: 85.7 us; the launch traced here: 85.5 us
  Pallas kernels  80 us (93%)
  local copies, waits for them, and re-layouts  4.2 us (5%)
    pallas_call x1, Pallas kernels, body(): pl.pallas_call(functools.partial(exchange_kernel, devices), out_shape=(ja...  29.3 us
    pallas_call x1, Pallas kernels, body(): pl.pallas_call(functools.partial(fluid_kernel, devices, cap), out_shape=(...  29.1 us
    pallas_call x1, Pallas kernels, body(): pl.pallas_call(functools.partial(spread_kernel, cap, ny), out_shape=jax.S...  17.9 us
    unnamed x13, local copies, waits for them, and re-layouts  3.97 us
    pallas_call x1, Pallas kernels, body(): pl.pallas_call(functools.partial(pack_kernel, cap), out_shape=(jax.ShapeD...  2.27 us

profile of v2, /device:TPU:0, one launch (start us, length us, event | category | flops | bytes accessed | tf_op | source)
XLA Modules:
  0.0 85.5 jit_solution(12949004121728252957)
XLA Ops:
  0.6 0.0 copy-start.3
  0.6 0.7 copy-done.3
  1.3 0.1 copy.10
  1.4 0.1 reshape.19.offset
  1.6 0.0 copy-start.2
  1.6 1.1 %copy.11.coords = f32[128,3,128]{2,1,0:T(4,128)S(1)} copy(f32[128,3,128]{2,0,1:T(8,128)} %param.6) | data formatting | bytes 393216 | tf_op args[1]
  2.7 0.0 copy-done.2
  2.7 0.0 copy-start.1
  2.7 0.0 copy-start
  2.7 0.1 copy.12.force
  2.9 0.5 copy-done.1
  3.4 2.3 %shard_map.68 = (f32[32,56,128]{2,1,0:T(8,128)S(1)}, s32[128]{0:T(128)S(1)}) custom-call(s32[128]{0:T(128)S(1)} %bitcast.1, s32[256]{0:T(256)S(1)} %reshape.19.offset, f32[128,3,128]{2,1,0:T(4,128)S(1)} %copy.11.coords, f32[128,3,128]{2,1,0:T(4,128)S(1)} %copy.12.force), custom_call_target="tpu_custom_call" | custom-call | tf_op jit(solution)/shard_map/pallas_call | solution.py:306
  5.6 0.0 copy-done
  5.6 29.3 %shard_map.69 = (f32[32,56,128]{2,1,0:T(8,128)S(1)}, f32[3,3,32,128]{3,2,1,0:T(8,128)S(1)}, f32[3,3,32,128]{3,2,1,0:T(8,128)S(1)}) custom-call(f32[32,56,128]{2,1,0:T(8,128)S(1)} %get-tuple-element.9.send, f32[3,8,32,128]{3,2,1,0:T(8,128)S(1)} %copy-done), custom_call_target="tpu_custom_call" | custom-call | tf_op jit(solution)/shard_map/pallas_call | solution.py:319
  34.9 0.6 clamp_reduce_fusion
  35.5 0.1 min.12.starts
  35.6 17.9 %shard_map.70.fmid = f32[8,32,128]{2,1,0:T(8,128)S(1)} custom-call(s32[256]{0:T(256)S(1)} %min.12.starts, f32[32,56,128]{2,1,0:T(8,128)S(1)} %get-tuple-element.10.rec), custom_call_target="tpu_custom_call" | custom-call | tf_op jit(solution)/shard_map/pallas_call | solution.py:338
  53.5 29.1 %shard_map.71 = (f32[3,8,32,128]{3,2,1,0:T(8,128)S(1)}, f32[32,24,128]{2,1,0:T(8,128)S(1)}) custom-call(s32[256]{0:T(256)S(1)} %min.12.starts, f32[3,8,32,128]{3,2,1,0:T(8,128)S(1)} %copy-done, f32[3,3,32,128]{3,2,1,0:T(8,128)S(1)} %get-tuple-element.11.vleft, f32[3,3,32,128]{3,2,1,0:T(8,128)S(1)} %get-tuple-element.12.vright, ...), custom_call_target="tpu_custom_call" | custom-call | tf_op jit(solution)/shard_map/pallas_call | solution.py:347
  82.6 1.5 %shard_map.72 = f32[128,3,128]{2,1,0:T(4,128)S(1)} custom-call(s32[128]{0:T(128)S(1)} %get-tuple-element.14.slots, f32[32,24,128]{2,1,0:T(8,128)S(1)} %get-tuple-element.15.got), custom_call_target="tpu_custom_call" | custom-call | tf_op jit(solution)/shard_map/pallas_call | solution.py:371
  84.1 0.7 copy.13
  84.8 0.7 copy.15
Async XLA Ops:
  0.6 0.7 copy-start.3
  1.6 1.1 %copy-start.2 = (f32[128,3,128]{2,0,1:T(8,128)S(1)}, f32[128,3,128]{2,0,1:T(8,128)}, u32[]{:S(2)}) copy-start(f32[128,3,128]{2,0,1:T(8,128)} %param.7) | copy-start | bytes 589828
  2.7 0.7 copy-start.1
  2.7 2.9 %copy-start = (f32[3,8,32,128]{3,2,1,0:T(8,128)S(1)}, f32[3,8,32,128]{3,2,1,0:T(8,128)}, u32[]{:S(2)}) copy-start(f32[3,8,32,128]{3,2,1,0:T(8,128)} %vel.3) | copy-start | bytes 1179652

commit v3 on v2

--- a/solution.py
+++ b/solution.py
@@ -63,14 +63,14 @@
         count[d] = r + 1
         slots[k] = d * cap + r
         for c in range(3):
-            send[d, pl.ds(c * cap + r, 1), :] = coords[k, c:c + 1, :]
-            send[d, pl.ds((3 + c) * cap + r, 1), :] = force[k, c:c + 1, :]
+            send[d, pl.ds(c * cap + r, 1), :] = coords[c, pl.ds(k, 1), :]
+            send[d, pl.ds((3 + c) * cap + r, 1), :] = force[c, pl.ds(k, 1), :]
         oy = offset[2 * k].astype(jnp.float32)
         oz = offset[2 * k + 1].astype(jnp.float32)
         send[d, pl.ds(6 * cap + r, 1), :] = jnp.where(lane == 0, oy, oz)
         return carry
 
-    lax.fori_loop(0, coords.shape[0], one, 0, unroll=4)
+    lax.fori_loop(0, coords.shape[1], one, 0, unroll=4)
 
 
 def spread_kernel(cap, ny, starts, rec, out, acc):
@@ -284,10 +284,10 @@
         d = slot // cap
         r = slot - d * cap
         for c in range(3):
-            out[k, c:c + 1, :] = got[d, pl.ds(c * cap + r, 1), :]
-        return carry
-
-    lax.fori_loop(0, out.shape[0], one, 0, unroll=4)
+            out[c, pl.ds(k, 1), :] = got[d, pl.ds(c * cap + r, 1), :]
+        return carry
+
+    lax.fori_loop(0, out.shape[1], one, 0, unroll=4)
 
 
 MESH = pl.DeviceIdType.MESH
@@ -313,7 +313,7 @@
         out_specs=(VMEM, SMEM),
         scratch_shapes=[pltpu.SMEM((devices,), jnp.int32)],
         compiler_params=PARAMS,
-    )(block_slab.reshape(blocks), block_offset.reshape(2 * blocks), node_coords, node_force)
+    )(block_slab.reshape(blocks), block_offset.reshape(2 * blocks), jnp.transpose(node_coords, (1, 0, 2)), jnp.transpose(node_force, (1, 0, 2)))
 
     halo = jax.ShapeDtypeStruct((3, 3, ny, nz), f32)
     rec, vleft, vright = pl.pallas_call(
@@ -370,12 +370,12 @@
 
     node_velocity = pl.pallas_call(
         functools.partial(unpack_kernel, cap),
-        out_shape=jax.ShapeDtypeStruct((blocks, 3, nodes), f32),
+        out_shape=jax.ShapeDtypeStruct((3, blocks, nodes), f32),
         in_specs=[SMEM, VMEM],
         out_specs=VMEM,
         compiler_params=PARAMS,
     )(slots, got)
-    return new, node_velocity
+    return new, jnp.transpose(node_velocity, (1, 0, 2))
 
 
 def solution(mesh):

time: 85.7 us -> 86.5 us (level)
    unnamed x13 -> x10, local copies, waits for them, and re-layouts: 3.97 us -> 4.09 us
where the time goes in v3:
time: 86.5 us; the launch traced here: 86.3 us
  Pallas kernels  80.7 us (93%)
  local copies, waits for them, and re-layouts  4.32 us (5%)
    pallas_call x1, Pallas kernels, body(): pl.pallas_call(functools.partial(exchange_kernel, devices), out_shape=(ja...  29.3 us
    pallas_call x1, Pallas kernels, body(): pl.pallas_call(functools.partial(fluid_kernel, devices, cap), out_shape=(...  29.1 us
    pallas_call x1, Pallas kernels, body(): pl.pallas_call(functools.partial(spread_kernel, cap, ny), out_shape=jax.S...  17.9 us
    unnamed x10, local copies, waits for them, and re-layouts  4.09 us
    pallas_call x1, Pallas kernels, body(): pl.pallas_call(functools.partial(pack_kernel, cap), out_shape=(jax.ShapeD...  2.27 us
    pallas_call x1, Pallas kernels, body(): pl.pallas_call(functools.partial(unpack_kernel, cap), out_shape=jax.Shape...  2.23 us

profile of v3, /device:TPU:0, one launch (start us, length us, event | category | flops | bytes accessed | tf_op | source)
XLA Modules:
  0.0 86.3 jit_solution(7623920031885739730)
XLA Ops:
  0.6 0.0 copy-start
  0.6 0.8 copy.7
  1.5 0.1 reshape.19.offset
  1.6 0.0 copy-start.1
  1.6 0.9 %copy-done.1 = f32[128,3,128]{2,0,1:T(8,128)S(1)} copy-done((f32[128,3,128]{2,0,1:T(8,128)S(1)}, f32[128,3,128]{2,0,1:T(8,128)}, u32[]{:S(2)}) %copy-start.1) | copy-done | bytes 196632
  2.5 0.0 copy-start.2
  2.5 0.9 %copy-done.2 = f32[128,3,128]{2,0,1:T(8,128)S(1)} copy-done((f32[128,3,128]{2,0,1:T(8,128)S(1)}, f32[128,3,128]{2,0,1:T(8,128)}, u32[]{:S(2)}) %copy-start.2) | copy-done | bytes 196632
  3.5 0.0 copy-start.3
  3.5 0.7 copy-done.3
  4.1 2.3 %shard_map.68 = (f32[32,56,128]{2,1,0:T(8,128)S(1)}, s32[128]{0:T(128)S(1)}) custom-call(s32[128]{0:T(128)S(1)} %bitcast.6, s32[256]{0:T(256)S(1)} %reshape.19.offset, f32[3,128,128]{2,1,0:T(8,128)S(1)} %bitcast.4, f32[3,128,128]{2,1,0:T(8,128)S(1)} %bitcast.5), custom_call_target="tpu_custom_call" | custom-call | tf_op jit(solution)/shard_map/pallas_call | solution.py:306
  6.4 0.0 copy-done
  6.4 29.3 %shard_map.69 = (f32[32,56,128]{2,1,0:T(8,128)S(1)}, f32[3,3,32,128]{3,2,1,0:T(8,128)S(1)}, f32[3,3,32,128]{3,2,1,0:T(8,128)S(1)}) custom-call(f32[32,56,128]{2,1,0:T(8,128)S(1)} %get-tuple-element.9.send, f32[3,8,32,128]{3,2,1,0:T(8,128)S(1)} %copy-done), custom_call_target="tpu_custom_call" | custom-call | tf_op jit(solution)/shard_map/pallas_call | solution.py:319
  35.7 0.6 clamp_reduce_fusion
  36.3 0.1 min.12.starts
  36.4 17.9 %shard_map.70.fmid = f32[8,32,128]{2,1,0:T(8,128)S(1)} custom-call(s32[256]{0:T(256)S(1)} %min.12.starts, f32[32,56,128]{2,1,0:T(8,128)S(1)} %get-tuple-element.10.rec), custom_call_target="tpu_custom_call" | custom-call | tf_op jit(solution)/shard_map/pallas_call | solution.py:338
  54.3 29.1 %shard_map.71 = (f32[3,8,32,128]{3,2,1,0:T(8,128)S(1)}, f32[32,24,128]{2,1,0:T(8,128)S(1)}) custom-call(s32[256]{0:T(256)S(1)} %min.12.starts, f32[3,8,32,128]{3,2,1,0:T(8,128)S(1)} %copy-done, f32[3,3,32,128]{3,2,1,0:T(8,128)S(1)} %get-tuple-element.11.vleft, f32[3,3,32,128]{3,2,1,0:T(8,128)S(1)} %get-tuple-element.12.vright, ...), custom_call_target="tpu_custom_call" | custom-call | tf_op jit(solution)/shard_map/pallas_call | solution.py:347
  83.3 2.2 %shard_map.72 = f32[3,128,128]{2,1,0:T(8,128)} custom-call(s32[128]{0:T(128)S(1)} %get-tuple-element.14.slots, f32[32,24,128]{2,1,0:T(8,128)S(1)} %get-tuple-element.15.got), custom_call_target="tpu_custom_call" | custom-call | tf_op jit(solution)/shard_map/pallas_call | solution.py:371
  85.6 0.7 copy.9
Async XLA Ops:
  0.6 5.8 %copy-start = (f32[3,8,32,128]{3,2,1,0:T(8,128)S(1)}, f32[3,8,32,128]{3,2,1,0:T(8,128)}, u32[]{:S(2)}) copy-start(f32[3,8,32,128]{3,2,1,0:T(8,128)} %vel.3) | copy-start | bytes 1179652
  1.6 0.9 %copy-start.1 = (f32[128,3,128]{2,0,1:T(8,128)S(1)}, f32[128,3,128]{2,0,1:T(8,128)}, u32[]{:S(2)}) copy-start(f32[128,3,128]{2,0,1:T(8,128)} %param.6) | copy-start | bytes 589828
  2.5 0.9 %copy-start.2 = (f32[128,3,128]{2,0,1:T(8,128)S(1)}, f32[128,3,128]{2,0,1:T(8,128)}, u32[]{:S(2)}) copy-start(f32[128,3,128]{2,0,1:T(8,128)} %param.7) | copy-start | bytes 589828
  3.5 0.7 copy-start.3
